TPU v7x, 32 devices: a whole 2x2x4 slice. The times are simulated.
32 devices in a mesh: chain: 4 (over x, core), wide: 8 (over z, y).
Axes of the slice: x: 2, y: 2, z: 4, core: 2. Of those that a mesh axis runs over, the one named last changes fastest.
Arguments:
- right_side: float32 [4, 64, 1024], P('chain', None, 'wide'), may hold values from -6 to 6
- lower_blocks: bfloat16 [4, 4, 64, 64, 1024], P('chain', None, None, None, 'wide'), may hold values from -1 to 1
- lower_index: int32 [4, 4, 1024], P('chain', None, 'wide'), may hold values from 0 to 1023
- upper_blocks: bfloat16 [4, 4, 64, 64, 1024], P('chain', None, None, None, 'wide'), may hold values from -1 to 1
- upper_index: int32 [4, 4, 1024], P('chain', None, 'wide'), may hold values from 0 to 1023
- inverse: bfloat16 [4, 64, 64, 1024], P('chain', None, None, 'wide'), may hold values from -0.5 to 1, as said below
- donor_weight: bfloat16 [4, 64, 64, 1024], P('chain', None, None, 'wide'), may hold values from -1 to 1
- donor_index: int32 [4, 1024], P('chain', 'wide'), may hold values from 0 to 1023
- target: int32 [4, 1024], P('chain', 'wide'), may hold values from 0 to 1023, as said below
Outputs:
- relocated: float32 [4, 64, 1024], P('chain', None, 'wide')
Inputs may be any that keep to these rules, and one draw needn't show every extreme that they name: `inverse`: inverses of well-conditioned pivot blocks. For each level set, a permutation of the block rows; block row b of wide index b // 128 goes to wide index target // 128; every wide index receives 128 block rows of a level set and hands at most 32 of them to any one wide index, exactly 32 to some.
All inputs are finite; a program needn't handle non-finite values.
Results may differ from a plain program's by a relative error of at most 0.007.
Values may be sent and summed in bfloat16 or wider, within the bound.
A program may use at most 64 MiB of HBM per device.

v0:
```python
import jax
import jax.numpy as jnp
from jax import lax
from jax.sharding import PartitionSpec as P


def passed_along(value, axis, steps):
    count = lax.axis_size(axis)
    first, last = (max(0, -steps), min(count, count - steps))
    return lax.ppermute(value, axis, [(source, source + steps) for source in range(first, last)])


def couple(blocks, index, gathered):
    picked = jnp.take(gathered, index, axis=1)
    return jnp.einsum("kijb,jkb->ib", blocks, picked, preferred_element_type=jnp.float32)


def apply_inverse(inverse_level, values):
    return jnp.einsum(
        "ijb,jb->ib", inverse_level, values.astype(jnp.bfloat16), preferred_element_type=jnp.float32
    )


def fetch_previous(solved):
    rounded = solved.astype(jnp.bfloat16)
    gathered = lax.all_gather(rounded, "wide", axis=1, tiled=True)
    return passed_along(gathered, "chain", 1)


def fetch_following(solved):
    rounded = solved.astype(jnp.bfloat16)
    gathered = lax.all_gather(rounded, "wide", axis=1, tiled=True)
    return passed_along(gathered, "chain", -1)


def per_device(
    right_side,
    lower_blocks,
    lower_index,
    upper_blocks,
    upper_index,
    inverse,
    donor_weight,
    donor_index,
    target,
):
    local_rhs = right_side[0]
    inverse_level = inverse[0]
    block_count = local_rhs.shape[1]
    unknowns = local_rhs.shape[0]
    level_rhs = lax.all_gather(local_rhs.astype(jnp.bfloat16), "wide", axis=1, tiled=True)
    donor_values = jnp.take(level_rhs, donor_index[0], axis=1)
    source = local_rhs + jnp.einsum(
        "ijb,jb->ib", donor_weight[0], donor_values, preferred_element_type=jnp.float32
    )
    forward = apply_inverse(inverse_level, source)
    for sweep in range(lax.axis_size("chain") - 1):
        previous = fetch_previous(forward)
        forward = apply_inverse(
            inverse_level, source - couple(lower_blocks[0], lower_index[0], previous)
        )
    solved = forward
    for sweep in range(lax.axis_size("chain") - 1):
        following = fetch_following(solved)
        solved = forward - apply_inverse(
            inverse_level, couple(upper_blocks[0], upper_index[0], following)
        )
    level_width = lax.axis_size("wide")
    places = target[0]
    capacity = block_count // 4
    owners = places // block_count
    slots = places % block_count
    onehot = (owners[:, None] == jnp.arange(level_width)[None, :]).astype(jnp.int32)
    running = jnp.cumsum(onehot, axis=0)
    within = jnp.sum(running * onehot, axis=1) - 1
    position = owners * capacity + within
    payload = jnp.zeros((unknowns, level_width * capacity), jnp.float32).at[:, position].set(solved)
    payload = payload.reshape(unknowns, level_width, capacity).transpose(1, 0, 2)
    labels = (
        jnp.full((level_width * capacity,), -1, jnp.int32)
        .at[position]
        .set(slots)
        .reshape(level_width, capacity)
    )
    arrived, arrived_labels = (
        lax.all_to_all(payload, "wide", split_axis=0, concat_axis=0, tiled=True),
        lax.all_to_all(labels, "wide", split_axis=0, concat_axis=0, tiled=True),
    )
    flat = arrived.transpose(1, 0, 2).reshape(unknowns, level_width * capacity)
    flat_labels = arrived_labels.reshape(level_width * capacity)
    spots = jnp.where(flat_labels >= 0, flat_labels, block_count)
    placed = jnp.zeros((unknowns, block_count + 1), jnp.float32).at[:, spots].set(flat)
    return placed[:, :block_count][None]


def solution(mesh):
    in_specs = (
        P("chain", None, "wide"),
        P("chain", None, None, None, "wide"),
        P("chain", None, "wide"),
        P("chain", None, None, None, "wide"),
        P("chain", None, "wide"),
        P("chain", None, None, "wide"),
        P("chain", None, None, "wide"),
        P("chain", "wide"),
        P("chain", "wide"),
    )
    out_specs = P("chain", None, "wide")
    return jax.shard_map(
        per_device, mesh=mesh, in_specs=in_specs, out_specs=out_specs, check_vma=False
    )
```

profile of v0, /device:TPU:2, one launch (start us, length us, event | category | flops | bytes accessed | tf_op | source)
XLA Modules:
  0.0 359.4 jit_solution(7254904002857355993)
XLA Ops:
  0.0 0.7 fusion.42
  0.8 0.7 compare_and_fusion.2
  1.4 4.7 %copy.16 = bf16[64,64,128]{0,1,2:T(8,128)(2,1)S(1)} copy(bf16[64,64,128]{2,1,0:T(8,128)(2,1)} %bitcast.202) | data formatting | bytes 2097152 | tf_op jit(solution)/shard_map/squeeze | solution.py:48
  6.3 31.1 %all_gather.21 = bf16[64,1024]{0,1:T(8,128)(2,1)S(1)} all-gather(bf16[64,128]{0,1:T(8,128)(2,1)S(1)} %bitcast_convert_fusion), channel_id=1, replica_groups=mesh['chain'=4,'wide'=8] {'wide'}, dimensions={1}, use_global_device_ids=true | all-gather | bytes 147456 | tf_op jit(solution)/shard_map/all_gather | solution.py:51
  37.3 4.5 %copy.13 = bf16[64,64,128]{0,1,2:T(8,128)(2,1)} copy(bf16[64,64,128]{2,1,0:T(8,128)(2,1)S(1)} %bitcast.203) | data formatting | bytes 2097152 | tf_op jit(solution)/shard_map/squeeze | solution.py:54
  41.8 0.7 gather_fusion
  42.7 2.2 fusion.26
  45.6 30.7 %all_gather.22 = bf16[64,1024]{0,1:T(8,128)(2,1)S(1)} all-gather(bf16[64,128]{0,1:T(8,128)(2,1)S(1)} %convert_bitcast_fusion.6), channel_id=1, replica_groups=mesh['chain'=4,'wide'=8] {'wide'}, dimensions={1}, use_global_device_ids=true | all-gather | bytes 147456 | tf_op jit(solution)/shard_map/all_gather | solution.py:26
  76.3 1.9 collective-permute-start
  78.3 15.6 %copy.19 = bf16[4,64,64,128]{1,2,0,3:T(8,128)(2,1)} copy(bf16[4,64,64,128]{3,2,1,0:T(8,128)(2,1)} %bitcast.200) | data formatting | bytes 8388608 | tf_op jit(solution)/shard_map/squeeze | solution.py:60
  93.9 1.3 gather_fusion.1
  95.4 4.7 %fusion.10 = f32[128,1,64,1]{2,1,3,0:T(1,128)S(1)} fusion(bf16[4,64,64,128]{1,2,0,3:T(8,128)(2,1)} %copy.19, bf16[64,4,128,1]{0,2,1,3:T(8,128)(2,1)S(1)} %select_bitcast_fusion.5), kind=kOutput, calls=%fused_computation.20 | convolution fusion | flops 4194304 | bytes 4292608 | tf_op jit(solution)/shard_map/kijb,jkb->ib/dot_general | solution.py:15
  100.9 30.7 %all_gather.23 = bf16[64,1024]{0,1:T(8,128)(2,1)S(1)} all-gather(bf16[64,128]{0,1:T(8,128)(2,1)S(1)} %convert_bitcast_fusion.5), channel_id=1, replica_groups=mesh['chain'=4,'wide'=8] {'wide'}, dimensions={1}, use_global_device_ids=true | all-gather | bytes 147456 | tf_op jit(solution)/shard_map/all_gather | solution.py:26
  131.6 1.9 collective-permute-start.1
  133.5 5.7 %collective-permute-done.1 = bf16[64,1024]{0,1:T(8,128)(2,1)S(1)} collective-permute-done((bf16[64,1024]{0,1:T(8,128)(2,1)S(1)}, bf16[64,1024]{0,1:T(8,128)(2,1)S(1)}, u32[]{:S(2)}, u32[]{:S(2)}) %collective-permute-start.1) | collective-permute-done | bytes 131104 | tf_op jit(solution)/shard_map/ppermute | solution.py:10
  139.3 1.3 gather_fusion.2
  140.8 4.7 %fusion.8 = f32[128,1,64,1]{2,1,3,0:T(1,128)S(1)} fusion(bf16[4,64,64,128]{1,2,0,3:T(8,128)(2,1)} %copy.19, bf16[64,4,128,1]{0,2,1,3:T(8,128)(2,1)S(1)} %select_bitcast_fusion.4), kind=kOutput, calls=%fused_computation.18 | convolution fusion | flops 4194304 | bytes 4292608 | tf_op jit(solution)/shard_map/kijb,jkb->ib/dot_general | solution.py:15
  146.2 30.9 %all_gather.24 = bf16[64,1024]{0,1:T(8,128)(2,1)S(1)} all-gather(bf16[64,128]{0,1:T(8,128)(2,1)S(1)} %convert_bitcast_fusion.4), channel_id=1, replica_groups=mesh['chain'=4,'wide'=8] {'wide'}, dimensions={1}, use_global_device_ids=true | all-gather | bytes 147456 | tf_op jit(solution)/shard_map/all_gather | solution.py:26
  177.0 2.1 collective-permute-start.2
  179.2 5.6 %collective-permute-done.2 = bf16[64,1024]{0,1:T(8,128)(2,1)S(1)} collective-permute-done((bf16[64,1024]{0,1:T(8,128)(2,1)S(1)}, bf16[64,1024]{0,1:T(8,128)(2,1)S(1)}, u32[]{:S(2)}, u32[]{:S(2)}) %collective-permute-start.2) | collective-permute-done | bytes 131104 | tf_op jit(solution)/shard_map/ppermute | solution.py:10
  184.7 1.3 gather_fusion.3
  186.2 4.7 %fusion.6 = f32[128,1,64,1]{2,1,3,0:T(1,128)S(1)} fusion(bf16[4,64,64,128]{1,2,0,3:T(8,128)(2,1)} %copy.19, bf16[64,4,128,1]{0,2,1,3:T(8,128)(2,1)S(1)} %select_bitcast_fusion.3), kind=kOutput, calls=%fused_computation.16 | convolution fusion | flops 4194304 | bytes 4292608 | tf_op jit(solution)/shard_map/kijb,jkb->ib/dot_general | solution.py:15
  191.6 30.9 %all_gather.25 = bf16[64,1024]{0,1:T(8,128)(2,1)S(1)} all-gather(bf16[64,128]{0,1:T(8,128)(2,1)S(1)} %convert_bitcast_fusion.3), channel_id=1, replica_groups=mesh['chain'=4,'wide'=8] {'wide'}, dimensions={1}, use_global_device_ids=true | all-gather | bytes 147456 | tf_op jit(solution)/shard_map/all_gather | solution.py:32
  222.5 1.9 collective-permute-start.3
  224.4 15.6 %copy.32 = bf16[4,64,64,128]{1,2,0,3:T(8,128)(2,1)} copy(bf16[4,64,64,128]{3,2,1,0:T(8,128)(2,1)} %bitcast.201) | data formatting | bytes 8388608 | tf_op jit(solution)/shard_map/squeeze | solution.py:66
  240.1 1.3 gather_fusion.4
  241.6 4.7 %fusion.4 = f32[128,1,64,1]{2,1,3,0:T(1,128)S(1)} fusion(bf16[4,64,64,128]{1,2,0,3:T(8,128)(2,1)} %copy.32, bf16[64,4,128,1]{0,2,1,3:T(8,128)(2,1)S(1)} %select_bitcast_fusion.2), kind=kOutput, calls=%fused_computation.14 | convolution fusion | flops 4194304 | bytes 4292608 | tf_op jit(solution)/shard_map/kijb,jkb->ib/dot_general | solution.py:15
  246.3 0.7 fusion.16
  247.0 30.7 %all_gather.26 = bf16[64,1024]{0,1:T(8,128)(2,1)S(1)} all-gather(bf16[64,128]{0,1:T(8,128)(2,1)S(1)} %fusion.37), channel_id=1, replica_groups=mesh['chain'=4,'wide'=8] {'wide'}, dimensions={1}, use_global_device_ids=true | all-gather | bytes 147456 | tf_op jit(solution)/shard_map/all_gather | solution.py:32
  277.8 1.9 collective-permute-start.4
  280.1 3.4 collective-permute-done.4
  283.6 1.3 gather_fusion.5
  285.0 4.7 %fusion.2 = f32[128,1,64,1]{2,1,3,0:T(1,128)S(1)} fusion(bf16[4,64,64,128]{1,2,0,3:T(8,128)(2,1)} %copy.32, bf16[64,4,128,1]{0,2,1,3:T(8,128)(2,1)S(1)} %select_bitcast_fusion.1), kind=kOutput, calls=%fused_computation.12 | convolution fusion | flops 4194304 | bytes 4292608 | tf_op jit(solution)/shard_map/kijb,jkb->ib/dot_general | solution.py:15
  289.8 0.7 fusion.14
  290.5 30.8 %all_gather.27 = bf16[64,1024]{0,1:T(8,128)(2,1)S(1)} all-gather(bf16[64,128]{0,1:T(8,128)(2,1)S(1)} %fusion.38), channel_id=1, replica_groups=mesh['chain'=4,'wide'=8] {'wide'}, dimensions={1}, use_global_device_ids=true | all-gather | bytes 147456 | tf_op jit(solution)/shard_map/all_gather | solution.py:32
  321.3 1.9 collective-permute-start.5
  323.3 1.0 scatter_custom_fusion
  324.3 11.7 %all_to_all.14 = s32[8,1,32]{2,1,0:T(1,128)S(1)} all-to-all(s32[8,1,32]{2,1,0:T(1,128)S(1)} %all_to_all.9), channel_id=1, replica_groups=mesh['chain'=4,'wide'=8] {'wide'}, dimensions={0} | all-to-all | bytes 2048 | tf_op jit(solution)/shard_map/all_to_all | solution.py:87
  337.3 1.3 gather_fusion.6
  338.8 4.7 %fusion = f32[128,1,64,1]{2,1,3,0:T(1,128)S(1)} fusion(bf16[4,64,64,128]{1,2,0,3:T(8,128)(2,1)} %copy.32, bf16[64,4,128,1]{0,2,1,3:T(8,128)(2,1)S(1)} %select_bitcast_fusion), kind=kOutput, calls=%fused_computation.10 | convolution fusion | flops 4194304 | bytes 4292608 | tf_op jit(solution)/shard_map/kijb,jkb->ib/dot_general | solution.py:15
  343.6 0.7 fusion.12
  344.2 0.9 scatter_custom_fusion.1
  345.2 0.7 reshape.346
  345.9 3.3 all-to-all-start.1
  349.3 6.8 %all-to-all-done.1 = f32[8,1,2048]{2,1,0:T(1,128)S(1)} async-done(((f32[8,1,2048]{2,1,0:T(1,128)}), f32[8,1,2048]{2,1,0:T(1,128)S(1)}, u32[]{:S(2)}, u32[]{:S(2)}) %all-to-all-start.1) | async-done | bytes 65568 | tf_op jit(solution)/shard_map/all_to_all | solution.py:86
  356.6 0.8 reduce.4
  357.5 1.1 scatter_custom_fusion.2
  358.7 0.7 copy.11
  (59 shorter events, 6.2 us)
Async XLA Ops:
  0.0 6.1 %copy-start.1 = (f32[1,64,128]{2,1,0:T(8,128)S(1)}, f32[1,64,128]{2,1,0:T(8,128)}, u32[]{:S(2)}) copy-start(f32[1,64,128]{2,1,0:T(8,128)} %param.11) | copy-start | bytes 98308
  0.0 37.3 %copy-start = (bf16[1,64,64,128]{3,2,1,0:T(8,128)(2,1)S(1)}, bf16[1,64,64,128]{3,2,1,0:T(8,128)(2,1)}, u32[]{:S(2)}) copy-start(bf16[1,64,64,128]{3,2,1,0:T(8,128)(2,1)} %param.17) | copy-start | bytes 3145732
  42.6 35.6 %copy-start.2 = (s32[1,4,128]{2,1,0:T(4,128)S(1)}, s32[1,4,128]{2,1,0:T(4,128)}, u32[]{:S(2)}) copy-start(s32[1,4,128]{2,1,0:T(4,128)} %param.13) | copy-start | bytes 6148
  76.3 17.6 %collective-permute-start = (bf16[64,1024]{0,1:T(8,128)(2,1)S(1)}, bf16[64,1024]{0,1:T(8,128)(2,1)S(1)}, u32[]{:S(2)}, u32[]{:S(2)}) collective-permute-start(bf16[64,1024]{0,1:T(8,128)(2,1)S(1)} %all_gather.22), channel_id=1, source_target_pairs={{0,8},{8,16},{16,24},{1,9},{9,17},{17,25},{2,10},{10,18},{18,26},{... | collective-permute-start | bytes 393224 | tf_op jit(solution)/shard_map/ppermute | solution.py:10
  100.2 33.3 %copy-start.3 = (s32[1,4,128]{2,1,0:T(4,128)S(1)}, s32[1,4,128]{2,1,0:T(4,128)}, u32[]{:S(2)}) copy-start(s32[1,4,128]{2,1,0:T(4,128)} %param.15) | copy-start | bytes 6148
  131.6 7.7 %collective-permute-start.1 = (bf16[64,1024]{0,1:T(8,128)(2,1)S(1)}, bf16[64,1024]{0,1:T(8,128)(2,1)S(1)}, u32[]{:S(2)}, u32[]{:S(2)}) collective-permute-start(bf16[64,1024]{0,1:T(8,128)(2,1)S(1)} %all_gather.23), channel_id=1, source_target_pairs={{0,8},{8,16},{16,24},{1,9},{9,17},{17,25},{2,10},{10,18},{18,26},{... | collective-permute-start | bytes 393224 | tf_op jit(solution)/shard_map/ppermute | solution.py:10
  177.0 7.7 %collective-permute-start.2 = (bf16[64,1024]{0,1:T(8,128)(2,1)S(1)}, bf16[64,1024]{0,1:T(8,128)(2,1)S(1)}, u32[]{:S(2)}, u32[]{:S(2)}) collective-permute-start(bf16[64,1024]{0,1:T(8,128)(2,1)S(1)} %all_gather.24), channel_id=1, source_target_pairs={{0,8},{8,16},{16,24},{1,9},{9,17},{17,25},{2,10},{10,18},{18,26},{... | collective-permute-start | bytes 393224 | tf_op jit(solution)/shard_map/ppermute | solution.py:10
  191.0 33.5 %copy-start.4 = (s32[1,128]{1,0:T(1,128)S(1)}, s32[1,128]{1,0:T(1,128)}, u32[]{:S(2)}) copy-start(s32[1,128]{1,0:T(1,128)} %param.19) | copy-start | bytes 1540
  222.5 17.6 %collective-permute-start.3 = (bf16[64,1024]{0,1:T(8,128)(2,1)S(1)}, bf16[64,1024]{0,1:T(8,128)(2,1)S(1)}, u32[]{:S(2)}, u32[]{:S(2)}) collective-permute-start(bf16[64,1024]{0,1:T(8,128)(2,1)S(1)} %all_gather.25), channel_id=1, source_target_pairs={{8,0},{16,8},{24,16},{9,1},{17,9},{25,17},{10,2},{18,10},{26,18},{... | collective-permute-start | bytes 393224 | tf_op jit(solution)/shard_map/ppermute | solution.py:10
  277.8 5.8 %collective-permute-start.4 = (bf16[64,1024]{0,1:T(8,128)(2,1)S(1)}, bf16[64,1024]{0,1:T(8,128)(2,1)S(1)}, u32[]{:S(2)}, u32[]{:S(2)}) collective-permute-start(bf16[64,1024]{0,1:T(8,128)(2,1)S(1)} %all_gather.26), channel_id=1, source_target_pairs={{8,0},{16,8},{24,16},{9,1},{17,9},{25,17},{10,2},{18,10},{26,18},{... | collective-permute-start | bytes 393224 | tf_op jit(solution)/shard_map/ppermute | solution.py:10
  321.3 16.0 %collective-permute-start.5 = (bf16[64,1024]{0,1:T(8,128)(2,1)S(1)}, bf16[64,1024]{0,1:T(8,128)(2,1)S(1)}, u32[]{:S(2)}, u32[]{:S(2)}) collective-permute-start(bf16[64,1024]{0,1:T(8,128)(2,1)S(1)} %all_gather.27), channel_id=1, source_target_pairs={{8,0},{16,8},{24,16},{9,1},{17,9},{25,17},{10,2},{18,10},{26,18},{... | collective-permute-start | bytes 393224 | tf_op jit(solution)/shard_map/ppermute | solution.py:10
  345.9 10.2 %all-to-all-start.1 = ((f32[8,1,2048]{2,1,0:T(1,128)}), f32[8,1,2048]{2,1,0:T(1,128)S(1)}, u32[]{:S(2)}, u32[]{:S(2)}) async-start(f32[8,1,2048]{2,1,0:T(1,128)} %reshape.346), calls=%async_computation.1 | async-start | bytes 131072 | tf_op jit(solution)/shard_map/all_to_all | solution.py:86
where the time goes:
time: 360 us; the launch traced here: 359 us
  blocking collectives  228 us (63%)
  local copies, waits for them, and re-layouts  54.2 us (15%)
  matrix products  35.3 us (10%)
  waiting for transfers between devices  21.6 us (6%)
  starting transfers between devices  15 us (4%)
  other arithmetic  5.35 us (1%)
    all_gather x3, blocking collectives, fetch_following(): gathered = lax.all_gather(rounded, 'wide', axis=1, tiled=True)  92.4 us
    all_gather x3, blocking collectives, fetch_previous(): gathered = lax.all_gather(rounded, 'wide', axis=1, tiled=True)  92.3 us
    all_gather x1, blocking collectives, per_device(): lax.all_gather(local_rhs.astype(jnp.bfloat16), 'wide', axis=1, tiled=True)  31.1 us
    dot_general x6, matrix products, couple(): jnp.einsum('kijb,jkb->ib', blocks, picked, preferred_element_type=jnp.flo...  28.5 us
    squeeze x1, local copies, waits for them, and re-layouts, per_device(): lower_blocks[0]  15.6 us
    squeeze x1, local copies, waits for them, and re-layouts, per_device(): upper_blocks[0]  15.6 us
    ppermute x6, waiting for transfers between devices, passed_along(): lax.ppermute(value, axis, [(source, source + steps) for source in range(f...  14.7 us
    all_to_all x1, blocking collectives, per_device(): lax.all_to_all(labels, 'wide', split_axis=0, concat_axis=0, tiled=True)  11.7 us
  transfers between devices with their start and end apart: 7, of which 4 were waited for; matrix products, arithmetic and copies ran while one was open for 9% of the time, Pallas kernels for 0%

commit v1 on v0

v1 whole, which is shorter than its diff:
```python
import functools

import jax
import jax.numpy as jnp
from jax import lax
from jax.experimental import pallas as pl
from jax.experimental.pallas import tpu as pltpu
from jax.sharding import PartitionSpec as P

MESH = pl.DeviceIdType.MESH
LANES = 128


def apply_blocks(blocks, vector, result):
    couples, rows, unknowns, width = blocks.shape
    group = 8

    def body(step, _):
        first = pl.multiple_of(step * group, group)
        total = jnp.zeros((group, 16, width), jnp.float32)
        for k in range(couples):
            for j in range(0, unknowns, 16):
                block = blocks[k, pl.ds(first, group), j : j + 16, :].astype(jnp.float32)
                total += block * vector[k, j : j + 16, :][None]
        result[pl.ds(first, group), :] = jnp.sum(total, axis=1)
        return 0

    lax.fori_loop(0, rows // group, body, 0)


def kernel(
    chain_count,
    wide_count,
    rhs,
    lower_hbm,
    lower_index,
    upper_hbm,
    upper_index,
    inverse_hbm,
    donor_hbm,
    donor_index,
    target,
    out,
    lower,
    upper,
    inverse,
    donor,
    rhs_all,
    forward_all,
    backward_all,
    final_all,
    target_all,
    rhs_send,
    forward_send,
    solved_send,
    picked,
    vector,
    product,
    source,
    forward,
    places,
    load_sem,
    send_sem,
    recv_sem,
):
    level = lax.axis_index("chain")
    me = lax.axis_index("wide")
    unknowns, width = source.shape

    loads = [
        pltpu.make_async_copy(hbm.at[0], vmem, load_sem.at[number])
        for number, (hbm, vmem) in enumerate(
            ((donor_hbm, donor.at[0]), (inverse_hbm, inverse.at[0]), (lower_hbm, lower), (upper_hbm, upper))
        )
    ]
    for load in loads:
        load.start()

    barrier = pltpu.get_barrier_semaphore()
    for step in range(1, wide_count):
        pl.semaphore_signal(
            barrier, inc=1, device_id=(level, lax.rem(me + step, wide_count)), device_id_type=MESH
        )

    @pl.when(level > 0)
    def _():
        for other in range(wide_count):
            pl.semaphore_signal(barrier, inc=1, device_id=(level - 1, other), device_id_type=MESH)

    @pl.when(level < chain_count - 1)
    def _():
        for other in range(wide_count):
            pl.semaphore_signal(barrier, inc=1, device_id=(level + 1, other), device_id_type=MESH)

    rhs_send[...] = rhs[0].astype(jnp.bfloat16)
    rhs_all[me] = rhs_send[...]
    target_all[me] = target[...]

    at_end = (level == 0) | (level == chain_count - 1)

    @pl.when(at_end)
    def _():
        pl.semaphore_wait(barrier, 2 * wide_count - 1)

    @pl.when(jnp.logical_not(at_end))
    def _():
        pl.semaphore_wait(barrier, 3 * wide_count - 1)

    def copy_to(value, gathered, phase, chain, other):
        return pltpu.make_async_remote_copy(
            src_ref=value,
            dst_ref=gathered.at[me],
            send_sem=send_sem.at[phase, other],
            recv_sem=recv_sem.at[phase, me],
            device_id=(chain, other),
            device_id_type=MESH,
        )

    def peers():
        return [lax.rem(me + step, wide_count) for step in range(1, wide_count)]

    def arrival(value, gathered, phase, other):
        return pltpu.make_async_remote_copy(
            src_ref=value,
            dst_ref=gathered.at[other],
            send_sem=send_sem.at[phase, other],
            recv_sem=recv_sem.at[phase, other],
            device_id=(level, other),
            device_id_type=MESH,
        )

    def send_across(value, gathered, phase):
        for other in peers():
            copy_to(value, gathered, phase, level, other).start()

    def sent_across(value, gathered, phase):
        for other in peers():
            copy_to(value, gathered, phase, level, other).wait_send()

    def arrive_across(value, gathered, phase):
        for other in peers():
            arrival(value, gathered, phase, other).wait_recv()

    def send_along(value, gathered, phase, chain):
        for step in range(wide_count):
            copy_to(value, gathered, phase, chain, lax.rem(me + step, wide_count)).start()

    def sent_along(value, gathered, phase, chain):
        for step in range(wide_count):
            copy_to(value, gathered, phase, chain, lax.rem(me + step, wide_count)).wait_send()

    def pick(gathered, index, arrive):
        couples = index.shape[0]
        lanes = [jnp.broadcast_to(index[k : k + 1] % LANES, (unknowns, width)) for k in range(couples)]
        tiles = [jnp.broadcast_to(index[k : k + 1] // LANES, (unknowns, width)) for k in range(couples)]
        for other in range(wide_count):
            arrive(other)
            tile = gathered[other].astype(jnp.float32)
            for k in range(couples):
                found = jnp.take_along_axis(tile, lanes[k], axis=1, mode="promise_in_bounds")
                if other == 0:
                    picked[k] = found
                else:
                    picked[k] = jnp.where(tiles[k] == other, found, picked[k])

    send_across(rhs_send, rhs_all, 0)
    send_across(target, target_all, 1)
    arrive_across(rhs_send, rhs_all, 0)
    pick(rhs_all, donor_index[...], lambda other: None)
    loads[0].wait()
    apply_blocks(donor, picked.at[0:1], product)
    source[...] = rhs[0] + product[...]
    loads[1].wait()
    loads[2].wait()

    @pl.when(level > 0)
    def _():
        pick(
            forward_all,
            lower_index[0],
            lambda other: arrival(forward_send, forward_all, 2, other).wait_recv(),
        )
        apply_blocks(lower, picked, product)
        source[...] -= product[...]

    vector[0] = source[...].astype(jnp.bfloat16).astype(jnp.float32)
    apply_blocks(inverse, vector, forward)
    loads[3].wait()

    @pl.when(level < chain_count - 1)
    def _():
        forward_send[...] = forward[...].astype(jnp.bfloat16)
        send_along(forward_send, forward_all, 2, level + 1)

    arrive_across(target, target_all, 1)
    spots = me * width + lax.broadcasted_iota(jnp.int32, (width, width), 0)
    for other in range(wide_count):
        hit = spots == jnp.broadcast_to(target_all[other], (width, width))
        places[:, other * width : (other + 1) * width] = jnp.where(hit, 1.0, 0.0).astype(jnp.bfloat16)

    @pl.when(level < chain_count - 1)
    def _():
        pick(
            backward_all,
            upper_index[0],
            lambda other: arrival(solved_send, backward_all, 3, other).wait_recv(),
        )
        apply_blocks(upper, picked, product)
        vector[0] = product[...].astype(jnp.bfloat16).astype(jnp.float32)
        apply_blocks(inverse, vector, product)
        forward[...] -= product[...]

    solved_send[...] = forward[...].astype(jnp.bfloat16)

    @pl.when(level > 0)
    def _():
        send_along(solved_send, backward_all, 3, level - 1)

    final_all[me] = solved_send[...]
    send_across(solved_send, final_all, 4)
    arrive_across(solved_send, final_all, 4)
    placed = jnp.zeros((unknowns, width), jnp.float32)
    for other in range(wide_count):
        placed += lax.dot_general(
            final_all[other],
            places[:, other * width : (other + 1) * width],
            (((1,), (1,)), ((), ())),
            preferred_element_type=jnp.float32,
        )
    out[0] = placed

    sent_across(rhs_send, rhs_all, 0)
    sent_across(target, target_all, 1)

    @pl.when(level < chain_count - 1)
    def _():
        sent_along(forward_send, forward_all, 2, level + 1)

    @pl.when(level > 0)
    def _():
        sent_along(solved_send, backward_all, 3, level - 1)

    sent_across(solved_send, final_all, 4)


def solution(mesh):
    in_specs = (
        P("chain", None, "wide"),
        P("chain", None, None, None, "wide"),
        P("chain", None, "wide"),
        P("chain", None, None, None, "wide"),
        P("chain", None, "wide"),
        P("chain", None, None, "wide"),
        P("chain", None, None, "wide"),
        P("chain", "wide"),
        P("chain", "wide"),
    )
    out_specs = P("chain", None, "wide")
    chain_count, wide_count = mesh.shape["chain"], mesh.shape["wide"]

    def per_device(rhs, lower, lower_index, upper, upper_index, inverse, donor, donor_index, target):
        _, couples, unknowns, _, width = lower.shape
        inside = pl.BlockSpec(memory_space=pltpu.VMEM)
        outside = pl.BlockSpec(memory_space=pl.ANY)
        tile16 = pltpu.VMEM((unknowns, width), jnp.bfloat16)
        tile32 = pltpu.VMEM((unknowns, width), jnp.float32)
        gathered = pltpu.VMEM((wide_count, unknowns, width), jnp.bfloat16)
        return pl.pallas_call(
            functools.partial(kernel, chain_count, wide_count),
            out_shape=jax.ShapeDtypeStruct(rhs.shape, jnp.float32),
            in_specs=[inside, outside, inside, outside, inside, outside, outside, inside, inside],
            out_specs=inside,
            scratch_shapes=[
                pltpu.VMEM((couples, unknowns, unknowns, width), jnp.bfloat16),
                pltpu.VMEM((couples, unknowns, unknowns, width), jnp.bfloat16),
                pltpu.VMEM((1, unknowns, unknowns, width), jnp.bfloat16),
                pltpu.VMEM((1, unknowns, unknowns, width), jnp.bfloat16),
                gathered,
                gathered,
                gathered,
                gathered,
                pltpu.VMEM((wide_count, 1, width), jnp.int32),
                tile16,
                tile16,
                tile16,
                pltpu.VMEM((couples, unknowns, width), jnp.float32),
                pltpu.VMEM((1, unknowns, width), jnp.float32),
                tile32,
                tile32,
                tile32,
                pltpu.VMEM((width, wide_count * width), jnp.bfloat16),
                pltpu.SemaphoreType.DMA((4,)),
                pltpu.SemaphoreType.DMA((5, wide_count)),
                pltpu.SemaphoreType.DMA((5, wide_count)),
            ],
            compiler_params=pltpu.CompilerParams(
                collective_id=0, has_side_effects=True, vmem_limit_bytes=63 * 1024 * 1024
            ),
        )(rhs, lower, lower_index, upper, upper_index, inverse, donor, donor_index, target)

    return jax.shard_map(
        per_device, mesh=mesh, in_specs=in_specs, out_specs=out_specs, check_vma=False
    )
```

time: 360 us -> 56.4 us (0.16)
  the two profiles are of different devices: /device:TPU:2 before, /device:TPU:0 now
where the time goes in v1:
time: 56.4 us; the launch traced here: 56.1 us
  Pallas kernels  54.8 us (97%)
  local copies, waits for them, and re-layouts  1.38 us (2%)
    pallas_call x1, Pallas kernels, per_device(): pl.pallas_call(functools.partial(kernel, chain_count, wide_count), out_sh...  54.8 us
    unnamed x1, local copies, waits for them, and re-layouts  1.38 us

profile of v1, /device:TPU:0, one launch (start us, length us, event | category | flops | bytes accessed | tf_op | source)
XLA Modules:
  0.0 56.1 jit_solution(17686012228349057217)
XLA Ops:
  0.0 54.8 %shard_map.91 = f32[1,64,128]{2,1,0:T(8,128)} custom-call(f32[1,64,128]{2,1,0:T(8,128)} %rhs.1, bf16[1,4,64,64,128]{4,3,2,1,0:T(8,128)(2,1)} %lower_hbm.1, s32[1,4,128]{2,1,0:T(4,128)} %lower_index.1, bf16[1,4,64,64,128]{4,3,2,1,0:T(8,128)(2,1)} %upper_hbm.1, s32[1,4,128]{2,1,0:T(4,128)} %upper_index.1, bf16[1,64,64,128]{3,2,1,0:T(8,128)(2,1)} %inverse_hbm.1, ...), custom_call_target="tpu_custom_call" | custom-call | tf_op jit(solution)/shard_map/pallas_call | solution.py:268
  54.8 1.4 %copy.11 = f32[1,64,128]{2,1,0:T(8,128)} copy(f32[1,64,128]{2,1,0:T(8,128)} %shard_map.91) | data formatting | bytes 65536

commit v2 on v1

--- a/solution.py
+++ b/solution.py
@@ -8,7 +8,6 @@
 from jax.sharding import PartitionSpec as P
 
 MESH = pl.DeviceIdType.MESH
-LANES = 128
 
 
 def apply_blocks(blocks, vector, result):
@@ -31,16 +30,21 @@
 def kernel(
     chain_count,
     wide_count,
-    rhs,
+    rhs_hbm,
     lower_hbm,
-    lower_index,
+    lower_index_hbm,
     upper_hbm,
-    upper_index,
+    upper_index_hbm,
     inverse_hbm,
     donor_hbm,
+    donor_index_hbm,
+    target_hbm,
+    out,
+    rhs,
+    lower_index,
+    upper_index,
     donor_index,
     target,
-    out,
     lower,
     upper,
     inverse,
@@ -59,6 +63,9 @@
     source,
     forward,
     places,
+    donor_chosen,
+    lower_chosen,
+    upper_chosen,
     load_sem,
     send_sem,
     recv_sem,
@@ -67,32 +74,54 @@
     me = lax.axis_index("wide")
     unknowns, width = source.shape
 
+    def partner(step):
+        other, digit = 0, 1
+        while digit < wide_count:
+            mine = lax.rem(me // digit, 2)
+            other = other + digit * (1 - mine if step & digit else mine)
+            digit *= 2
+        return other
+
+    everyone = [partner(step) for step in range(wide_count)]
+    peers = everyone[1:]
+
+    barrier = pltpu.get_barrier_semaphore()
+
+    @pl.when(level > 0)
+    def _():
+        for other in reversed(everyone):
+            pl.semaphore_signal(barrier, inc=1, device_id=(level - 1, other), device_id_type=MESH)
+
+    @pl.when(level < chain_count - 1)
+    def _():
+        for other in reversed(everyone):
+            pl.semaphore_signal(barrier, inc=1, device_id=(level + 1, other), device_id_type=MESH)
+
+    for other in reversed(peers):
+        pl.semaphore_signal(barrier, inc=1, device_id=(level, other), device_id_type=MESH)
+
     loads = [
-        pltpu.make_async_copy(hbm.at[0], vmem, load_sem.at[number])
-        for number, (hbm, vmem) in enumerate(
-            ((donor_hbm, donor.at[0]), (inverse_hbm, inverse.at[0]), (lower_hbm, lower), (upper_hbm, upper))
+        pltpu.make_async_copy(outer, inner, load_sem.at[number])
+        for number, (outer, inner) in enumerate(
+            (
+                (rhs_hbm.at[0], rhs),
+                (target_hbm, target),
+                (donor_index_hbm, donor_index),
+                (donor_hbm.at[0], donor.at[0]),
+                (lower_index_hbm.at[0], lower_index),
+                (upper_index_hbm.at[0], upper_index),
+                (inverse_hbm.at[0], inverse.at[0]),
+                (lower_hbm.at[0], lower),
+                (upper_hbm.at[0], upper),
+            )
         )
     ]
     for load in loads:
         load.start()
 
-    barrier = pltpu.get_barrier_semaphore()
-    for step in range(1, wide_count):
-        pl.semaphore_signal(
-            barrier, inc=1, device_id=(level, lax.rem(me + step, wide_count)), device_id_type=MESH
-        )
-
-    @pl.when(level > 0)
-    def _():
-        for other in range(wide_count):
-            pl.semaphore_signal(barrier, inc=1, device_id=(level - 1, other), device_id_type=MESH)
-
-    @pl.when(level < chain_count - 1)
-    def _():
-        for other in range(wide_count):
-            pl.semaphore_signal(barrier, inc=1, device_id=(level + 1, other), device_id_type=MESH)
-
-    rhs_send[...] = rhs[0].astype(jnp.bfloat16)
+    loads[0].wait()
+    loads[1].wait()
+    rhs_send[...] = rhs[...].astype(jnp.bfloat16)
     rhs_all[me] = rhs_send[...]
     target_all[me] = target[...]
 
@@ -116,9 +145,6 @@
             device_id_type=MESH,
         )
 
-    def peers():
-        return [lax.rem(me + step, wide_count) for step in range(1, wide_count)]
-
     def arrival(value, gathered, phase, other):
         return pltpu.make_async_remote_copy(
             src_ref=value,
@@ -130,62 +156,73 @@
         )
 
     def send_across(value, gathered, phase):
-        for other in peers():
+        for other in reversed(peers):
             copy_to(value, gathered, phase, level, other).start()
 
     def sent_across(value, gathered, phase):
-        for other in peers():
+        for other in peers:
             copy_to(value, gathered, phase, level, other).wait_send()
 
     def arrive_across(value, gathered, phase):
-        for other in peers():
+        for other in peers:
             arrival(value, gathered, phase, other).wait_recv()
 
     def send_along(value, gathered, phase, chain):
-        for step in range(wide_count):
-            copy_to(value, gathered, phase, chain, lax.rem(me + step, wide_count)).start()
+        for other in reversed(everyone):
+            copy_to(value, gathered, phase, chain, other).start()
 
     def sent_along(value, gathered, phase, chain):
-        for step in range(wide_count):
-            copy_to(value, gathered, phase, chain, lax.rem(me + step, wide_count)).wait_send()
-
-    def pick(gathered, index, arrive):
-        couples = index.shape[0]
-        lanes = [jnp.broadcast_to(index[k : k + 1] % LANES, (unknowns, width)) for k in range(couples)]
-        tiles = [jnp.broadcast_to(index[k : k + 1] // LANES, (unknowns, width)) for k in range(couples)]
-        for other in range(wide_count):
-            arrive(other)
-            tile = gathered[other].astype(jnp.float32)
-            for k in range(couples):
-                found = jnp.take_along_axis(tile, lanes[k], axis=1, mode="promise_in_bounds")
-                if other == 0:
-                    picked[k] = found
-                else:
-                    picked[k] = jnp.where(tiles[k] == other, found, picked[k])
+        for other in everyone:
+            copy_to(value, gathered, phase, chain, other).wait_send()
+
+    def choose(index, chosen):
+        for k in range(index.shape[0]):
+            wanted = jnp.broadcast_to(index[k : k + 1], (width, width))
+            for other in range(wide_count):
+                columns = other * width + lax.broadcasted_iota(jnp.int32, (width, width), 0)
+                chosen[other, :, k * width : (k + 1) * width] = jnp.where(
+                    columns == wanted, 1.0, 0.0
+                ).astype(jnp.bfloat16)
+
+    def pick(gathered, chosen, arrive):
+        couples = chosen.shape[2] // width
+        total = jnp.zeros((unknowns, couples * width), jnp.float32)
+        for step, other in enumerate(everyone):
+            arrive(step, other)
+            total += jnp.dot(gathered[other], chosen[other], preferred_element_type=jnp.float32)
+        for k in range(couples):
+            picked[k] = total[:, k * width : (k + 1) * width]
 
     send_across(rhs_send, rhs_all, 0)
     send_across(target, target_all, 1)
-    arrive_across(rhs_send, rhs_all, 0)
-    pick(rhs_all, donor_index[...], lambda other: None)
-    loads[0].wait()
+    loads[2].wait()
+
+    def arrive_rhs(step, other):
+        if step > 0:
+            arrival(rhs_send, rhs_all, 0, other).wait_recv()
+
+    choose(donor_index[...], donor_chosen)
+    pick(rhs_all, donor_chosen, arrive_rhs)
+    loads[3].wait()
     apply_blocks(donor, picked.at[0:1], product)
-    source[...] = rhs[0] + product[...]
-    loads[1].wait()
-    loads[2].wait()
+    source[...] = rhs[...] + product[...]
+    for load in loads[4:8]:
+        load.wait()
 
     @pl.when(level > 0)
     def _():
+        choose(lower_index[...], lower_chosen)
         pick(
             forward_all,
-            lower_index[0],
-            lambda other: arrival(forward_send, forward_all, 2, other).wait_recv(),
+            lower_chosen,
+            lambda step, other: arrival(forward_send, forward_all, 2, other).wait_recv(),
         )
         apply_blocks(lower, picked, product)
         source[...] -= product[...]
 
     vector[0] = source[...].astype(jnp.bfloat16).astype(jnp.float32)
     apply_blocks(inverse, vector, forward)
-    loads[3].wait()
+    loads[8].wait()
 
     @pl.when(level < chain_count - 1)
     def _():
@@ -196,14 +233,15 @@
     spots = me * width + lax.broadcasted_iota(jnp.int32, (width, width), 0)
     for other in range(wide_count):
         hit = spots == jnp.broadcast_to(target_all[other], (width, width))
-        places[:, other * width : (other + 1) * width] = jnp.where(hit, 1.0, 0.0).astype(jnp.bfloat16)
+        places[other] = jnp.where(hit, 1.0, 0.0).astype(jnp.bfloat16)
 
     @pl.when(level < chain_count - 1)
     def _():
+        choose(upper_index[...], upper_chosen)
         pick(
             backward_all,
-            upper_index[0],
-            lambda other: arrival(solved_send, backward_all, 3, other).wait_recv(),
+            upper_chosen,
+            lambda step, other: arrival(solved_send, backward_all, 3, other).wait_recv(),
         )
         apply_blocks(upper, picked, product)
         vector[0] = product[...].astype(jnp.bfloat16).astype(jnp.float32)
@@ -218,12 +256,13 @@
 
     final_all[me] = solved_send[...]
     send_across(solved_send, final_all, 4)
-    arrive_across(solved_send, final_all, 4)
     placed = jnp.zeros((unknowns, width), jnp.float32)
-    for other in range(wide_count):
+    for step, other in enumerate(everyone):
+        if step > 0:
+            arrival(solved_send, final_all, 4, other).wait_recv()
         placed += lax.dot_general(
             final_all[other],
-            places[:, other * width : (other + 1) * width],
+            places[other],
             (((1,), (1,)), ((), ())),
             preferred_element_type=jnp.float32,
         )
@@ -268,9 +307,14 @@
         return pl.pallas_call(
             functools.partial(kernel, chain_count, wide_count),
             out_shape=jax.ShapeDtypeStruct(rhs.shape, jnp.float32),
-            in_specs=[inside, outside, inside, outside, inside, outside, outside, inside, inside],
+            in_specs=[outside] * 9,
             out_specs=inside,
             scratch_shapes=[
+                tile32,
+                pltpu.VMEM((couples, width), jnp.int32),
+                pltpu.VMEM((couples, width), jnp.int32),
+                pltpu.VMEM((1, width), jnp.int32),
+                pltpu.VMEM((1, width), jnp.int32),
                 pltpu.VMEM((couples, unknowns, unknowns, width), jnp.bfloat16),
                 pltpu.VMEM((couples, unknowns, unknowns, width), jnp.bfloat16),
                 pltpu.VMEM((1, unknowns, unknowns, width), jnp.bfloat16),
@@ -288,8 +332,11 @@
                 tile32,
                 tile32,
                 tile32,
-                pltpu.VMEM((width, wide_count * width), jnp.bfloat16),
-                pltpu.SemaphoreType.DMA((4,)),
+                pltpu.VMEM((wide_count, width, width), jnp.bfloat16),
+                pltpu.VMEM((wide_count, width, width), jnp.bfloat16),
+                pltpu.VMEM((wide_count, width, couples * width), jnp.bfloat16),
+                pltpu.VMEM((wide_count, width, couples * width), jnp.bfloat16),
+                pltpu.SemaphoreType.DMA((9,)),
                 pltpu.SemaphoreType.DMA((5, wide_count)),
                 pltpu.SemaphoreType.DMA((5, wide_count)),
             ],

time: 56.4 us -> 53.3 us (0.945)
  Pallas kernels: 54.8 us -> 51.8 us
    pallas_call x1, Pallas kernels: 54.8 us -> 51.8 us  [per_device(): pl.pallas_call(functools.partial(kernel, chain_count, wide_count), out_sh...]
where the time goes in v2:
time: 53.3 us; the launch traced here: 53.1 us
  Pallas kernels  51.8 us (97%)
  local copies, waits for them, and re-layouts  1.38 us (3%)
    pallas_call x1, Pallas kernels, per_device(): pl.pallas_call(functools.partial(kernel, chain_count, wide_count), out_sh...  51.8 us
    unnamed x1, local copies, waits for them, and re-layouts  1.38 us

profile of v2, /device:TPU:0, one launch (start us, length us, event | category | flops | bytes accessed | tf_op | source)
XLA Modules:
  0.0 53.1 jit_solution(13143586084416115363)
XLA Ops:
  0.0 51.8 %shard_map.91 = f32[1,64,128]{2,1,0:T(8,128)} custom-call(f32[1,64,128]{2,1,0:T(8,128)} %rhs_hbm.1, bf16[1,4,64,64,128]{4,3,2,1,0:T(8,128)(2,1)} %lower_hbm.1, s32[1,4,128]{2,1,0:T(4,128)} %lower_index_hbm.1, bf16[1,4,64,64,128]{4,3,2,1,0:T(8,128)(2,1)} %upper_hbm.1, s32[1,4,128]{2,1,0:T(4,128)} %upper_index_hbm.1, bf16[1,64,64,128]{3,2,1,0:T(8,128)(2,1)} %inverse_hbm.1, ...), custom_call_target="tpu_custom_call" | custom-call | tf_op jit(solution)/shard_map/pallas_call | solution.py:307
  51.8 1.4 %copy.11 = f32[1,64,128]{2,1,0:T(8,128)} copy(f32[1,64,128]{2,1,0:T(8,128)} %shard_map.91) | data formatting | bytes 65536

commit v3 on v2

--- a/solution.py
+++ b/solution.py
@@ -10,7 +10,7 @@
 MESH = pl.DeviceIdType.MESH
 
 
-def apply_blocks(blocks, vector, result):
+def apply_blocks(blocks, vector, result, part=0, parts=1):
     couples, rows, unknowns, width = blocks.shape
     group = 8
 
@@ -24,7 +24,8 @@
         result[pl.ds(first, group), :] = jnp.sum(total, axis=1)
         return 0
 
-    lax.fori_loop(0, rows // group, body, 0)
+    steps = rows // group // parts
+    lax.fori_loop(part * steps, (part + 1) * steps, body, 0)
 
 
 def kernel(
@@ -167,13 +168,40 @@
         for other in peers:
             arrival(value, gathered, phase, other).wait_recv()
 
-    def send_along(value, gathered, phase, chain):
+    def half_to(value, gathered, phase, chain, other, half):
+        rows = pl.ds(half * (unknowns // 2), unknowns // 2)
+        return pltpu.make_async_remote_copy(
+            src_ref=value.at[rows],
+            dst_ref=gathered.at[me, rows],
+            send_sem=send_sem.at[phase + half, other],
+            recv_sem=recv_sem.at[phase + half, me],
+            device_id=(chain, other),
+            device_id_type=MESH,
+        )
+
+    def half_from(value, gathered, phase, other, half):
+        rows = pl.ds(half * (unknowns // 2), unknowns // 2)
+        return pltpu.make_async_remote_copy(
+            src_ref=value.at[rows],
+            dst_ref=gathered.at[other, rows],
+            send_sem=send_sem.at[phase + half, other],
+            recv_sem=recv_sem.at[phase + half, other],
+            device_id=(level, other),
+            device_id_type=MESH,
+        )
+
+    def send_along(value, gathered, phase, chain, half):
         for other in reversed(everyone):
-            copy_to(value, gathered, phase, chain, other).start()
+            half_to(value, gathered, phase, chain, other, half).start()
 
     def sent_along(value, gathered, phase, chain):
-        for other in everyone:
-            copy_to(value, gathered, phase, chain, other).wait_send()
+        for half in range(2):
+            for other in everyone:
+                half_to(value, gathered, phase, chain, other, half).wait_send()
+
+    def arrive_along(value, gathered, phase, other):
+        for half in range(2):
+            half_from(value, gathered, phase, other, half).wait_recv()
 
     def choose(index, chosen):
         for k in range(index.shape[0]):
@@ -193,6 +221,13 @@
         for k in range(couples):
             picked[k] = total[:, k * width : (k + 1) * width]
 
+    def find_places():
+        arrive_across(target, target_all, 1)
+        spots = me * width + lax.broadcasted_iota(jnp.int32, (width, width), 0)
+        for other in range(wide_count):
+            hit = spots == jnp.broadcast_to(target_all[other], (width, width))
+            places[other] = jnp.where(hit, 1.0, 0.0).astype(jnp.bfloat16)
+
     send_across(rhs_send, rhs_all, 0)
     send_across(target, target_all, 1)
     loads[2].wait()
@@ -212,28 +247,30 @@
     @pl.when(level > 0)
     def _():
         choose(lower_index[...], lower_chosen)
+        find_places()
         pick(
             forward_all,
             lower_chosen,
-            lambda step, other: arrival(forward_send, forward_all, 2, other).wait_recv(),
+            lambda step, other: arrive_along(forward_send, forward_all, 2, other),
         )
         apply_blocks(lower, picked, product)
         source[...] -= product[...]
 
     vector[0] = source[...].astype(jnp.bfloat16).astype(jnp.float32)
-    apply_blocks(inverse, vector, forward)
+    for half in range(2):
+        apply_blocks(inverse, vector, forward, half, 2)
+        rows = slice(half * (unknowns // 2), (half + 1) * (unknowns // 2))
+        forward_send[rows] = forward[rows].astype(jnp.bfloat16)
+
+        @pl.when(level < chain_count - 1)
+        def _():
+            send_along(forward_send, forward_all, 2, level + 1, half)
+
     loads[8].wait()
 
-    @pl.when(level < chain_count - 1)
-    def _():
-        forward_send[...] = forward[...].astype(jnp.bfloat16)
-        send_along(forward_send, forward_all, 2, level + 1)
-
-    arrive_across(target, target_all, 1)
-    spots = me * width + lax.broadcasted_iota(jnp.int32, (width, width), 0)
-    for other in range(wide_count):
-        hit = spots == jnp.broadcast_to(target_all[other], (width, width))
-        places[other] = jnp.where(hit, 1.0, 0.0).astype(jnp.bfloat16)
+    @pl.when(level == 0)
+    def _():
+        find_places()
 
     @pl.when(level < chain_count - 1)
     def _():
@@ -241,25 +278,31 @@
         pick(
             backward_all,
             upper_chosen,
-            lambda step, other: arrival(solved_send, backward_all, 3, other).wait_recv(),
+            lambda step, other: arrive_along(solved_send, backward_all, 4, other),
         )
         apply_blocks(upper, picked, product)
         vector[0] = product[...].astype(jnp.bfloat16).astype(jnp.float32)
-        apply_blocks(inverse, vector, product)
-        forward[...] -= product[...]
-
-    solved_send[...] = forward[...].astype(jnp.bfloat16)
-
-    @pl.when(level > 0)
-    def _():
-        send_along(solved_send, backward_all, 3, level - 1)
+
+    for half in range(2):
+        rows = slice(half * (unknowns // 2), (half + 1) * (unknowns // 2))
+
+        @pl.when(level < chain_count - 1)
+        def _():
+            apply_blocks(inverse, vector, product, half, 2)
+            forward[rows] -= product[rows]
+
+        solved_send[rows] = forward[rows].astype(jnp.bfloat16)
+
+        @pl.when(level > 0)
+        def _():
+            send_along(solved_send, backward_all, 4, level - 1, half)
 
     final_all[me] = solved_send[...]
-    send_across(solved_send, final_all, 4)
+    send_across(solved_send, final_all, 6)
     placed = jnp.zeros((unknowns, width), jnp.float32)
     for step, other in enumerate(everyone):
         if step > 0:
-            arrival(solved_send, final_all, 4, other).wait_recv()
+            arrival(solved_send, final_all, 6, other).wait_recv()
         placed += lax.dot_general(
             final_all[other],
             places[other],
@@ -277,9 +320,9 @@
 
     @pl.when(level > 0)
     def _():
-        sent_along(solved_send, backward_all, 3, level - 1)
-
-    sent_across(solved_send, final_all, 4)
+        sent_along(solved_send, backward_all, 4, level - 1)
+
+    sent_across(solved_send, final_all, 6)
 
 
 def solution(mesh):
@@ -337,8 +380,8 @@
                 pltpu.VMEM((wide_count, width, couples * width), jnp.bfloat16),
                 pltpu.VMEM((wide_count, width, couples * width), jnp.bfloat16),
                 pltpu.SemaphoreType.DMA((9,)),
-                pltpu.SemaphoreType.DMA((5, wide_count)),
-                pltpu.SemaphoreType.DMA((5, wide_count)),
+                pltpu.SemaphoreType.DMA((7, wide_count)),
+                pltpu.SemaphoreType.DMA((7, wide_count)),
             ],
             compiler_params=pltpu.CompilerParams(
                 collective_id=0, has_side_effects=True, vmem_limit_bytes=63 * 1024 * 1024

time: 53.3 us -> 52.5 us (0.985)
  Pallas kernels: 51.8 us -> 51 us
    pallas_call x1, Pallas kernels: 51.8 us -> 51 us  [per_device(): pl.pallas_call(functools.partial(kernel, chain_count, wide_count), out_sh...]
where the time goes in v3:
time: 52.5 us; the launch traced here: 52.4 us
  Pallas kernels  51 us (97%)
  local copies, waits for them, and re-layouts  1.38 us (3%)
    pallas_call x1, Pallas kernels, per_device(): pl.pallas_call(functools.partial(kernel, chain_count, wide_count), out_sh...  51 us
    unnamed x1, local copies, waits for them, and re-layouts  1.38 us

profile of v3, /device:TPU:0, one launch (start us, length us, event | category | flops | bytes accessed | tf_op | source)
XLA Modules:
  0.0 52.4 jit_solution(7262530929143289478)
XLA Ops:
  0.0 51.0 %shard_map.91 = f32[1,64,128]{2,1,0:T(8,128)} custom-call(f32[1,64,128]{2,1,0:T(8,128)} %rhs_hbm.1, bf16[1,4,64,64,128]{4,3,2,1,0:T(8,128)(2,1)} %lower_hbm.1, s32[1,4,128]{2,1,0:T(4,128)} %lower_index_hbm.1, bf16[1,4,64,64,128]{4,3,2,1,0:T(8,128)(2,1)} %upper_hbm.1, s32[1,4,128]{2,1,0:T(4,128)} %upper_index_hbm.1, bf16[1,64,64,128]{3,2,1,0:T(8,128)(2,1)} %inverse_hbm.1, ...), custom_call_target="tpu_custom_call" | custom-call | tf_op jit(solution)/shard_map/pallas_call | solution.py:350
  51.0 1.4 %copy.11 = f32[1,64,128]{2,1,0:T(8,128)} copy(f32[1,64,128]{2,1,0:T(8,128)} %shard_map.91) | data formatting | bytes 65536
